TPU v7x, 32 devices: a whole 2x2x4 slice. The times are simulated.
32 devices in a mesh: section: 2 (over x), expert: 16 (over z, y, core).
Axes of the slice: x: 2, y: 2, z: 4, core: 2. Of those that a mesh axis runs over, the one named last changes fastest.
Arguments:
- fwd_act: bfloat16 [2, 1024, 3584], P('section', 'expert'), may hold values from -6 to 6
- fwd_route: int32 [2, 1024], P('section', 'expert'), may hold values from 0 to 3, as said below
- fwd_weight: float32 [2, 1024], P('section', 'expert'), may hold values from 0.5 to 2.5
- bwd_act: bfloat16 [2, 1024, 3584], P('section', 'expert'), may hold values from -6 to 6
- bwd_grad: bfloat16 [2, 1024, 3584], P('section', 'expert'), may hold values from -6 to 6
- bwd_route: int32 [2, 1024], P('section', 'expert'), may hold values from 0 to 3, as said below
- bwd_weight: float32 [2, 1024], P('section', 'expert'), may hold values from 0.5 to 2.5
- w_gate: bfloat16 [2, 3584, 2048], P('section', None, 'expert'), may hold values from -0.09375 to 0.09375
- w_up: bfloat16 [2, 3584, 2048], P('section', None, 'expert'), may hold values from -0.09375 to 0.09375
- w_down: bfloat16 [2, 2048, 3584], P('section', 'expert'), may hold values from -0.1875 to 0.1875
Outputs:
- mixed: bfloat16 [2, 1024, 3584], P('section', 'expert')
- input_grad: bfloat16 [2, 1024, 3584], P('section', 'expert')
- gate_grad: float32 [2, 1024], P('section', 'expert')
Inputs may be any that keep to these rules, and one draw needn't show every extreme that they name: `fwd_route`: in the 64 tokens of one device no id occurs more than 24 times; in each section one id below 2 occurs exactly 24 times in the tokens of every device of that section. `bwd_route`: as for fwd_route.
All inputs are finite; a program needn't handle non-finite values.
Results may differ from a plain program's by a relative error of at most 0.0095.
Values may be sent and summed in bfloat16 or wider, within the bound.
A program may use at most 64 MiB of HBM per device.

v0:
```python
import jax
import jax.numpy as jnp
from jax import lax
from jax.sharding import PartitionSpec as P

FF = 1024


def passed_along(block, axis, distance):
    devices = range(lax.axis_size(axis))
    route = [((i - distance) % len(devices), i) for i in devices]
    return lax.ppermute(block, axis, route)


def route_plan(route_ids, experts, capacity):
    route_range = jnp.arange(2 * experts, dtype=jnp.int32)
    onehot = (route_ids[:, None] == route_range[None, :]).astype(jnp.int32)
    before = jnp.cumsum(onehot, axis=0) - onehot
    slot_ids = jnp.sum(before * onehot, axis=1)
    inside = route_ids < experts
    expert_ids = jnp.arange(experts, dtype=jnp.int32)
    slot_range = jnp.arange(capacity, dtype=jnp.int32)
    select = (
        (route_ids[None, None, :] == expert_ids[:, None, None])
        & (slot_ids[None, None, :] == slot_range[None, :, None])
    ).astype(jnp.bfloat16)
    place_at = jnp.where(inside, route_ids * capacity + slot_ids, 0)
    return (select, place_at, inside)


def pack_rows(select, token_rows, group_size):
    packed = jnp.einsum(
        "ect,td->ecd", select, token_rows, preferred_element_type=jnp.float32
    ).astype(jnp.bfloat16)
    copies = jnp.broadcast_to(packed[:, None], (packed.shape[0], group_size) + packed.shape[1:])
    return copies.reshape((packed.shape[0] * group_size,) + packed.shape[1:])


def unpack_sum(returned, group_size, place_at, inside):
    grouped = returned.astype(jnp.float32).reshape(
        (returned.shape[0] // group_size, group_size) + returned.shape[1:]
    )
    summed = jnp.sum(grouped, axis=1)
    flat = summed.reshape((summed.shape[0] * summed.shape[1],) + summed.shape[2:])
    picked = flat[place_at]
    mask = inside.reshape(inside.shape + (1,) * (picked.ndim - 1))
    return jnp.where(mask, picked, 0.0)


def expert_forward(token_rows, gate_cols, up_cols, down_rows):
    gate_pre = jnp.einsum("scd,dh->sch", token_rows, gate_cols, preferred_element_type=jnp.float32)
    up_pre = jnp.einsum("scd,dh->sch", token_rows, up_cols, preferred_element_type=jnp.float32)
    hidden = (jax.nn.silu(gate_pre) * up_pre).astype(jnp.bfloat16)
    return jnp.einsum("sch,hd->scd", hidden, down_rows, preferred_element_type=jnp.float32).astype(
        jnp.bfloat16
    )


def expert_backward(token_rows, grad_rows, gate_cols, up_cols, down_rows):
    gate_pre = jnp.einsum("scd,dh->sch", token_rows, gate_cols, preferred_element_type=jnp.float32)
    up_pre = jnp.einsum("scd,dh->sch", token_rows, up_cols, preferred_element_type=jnp.float32)
    gate_sig = jax.nn.sigmoid(gate_pre)
    active = gate_pre * gate_sig
    hidden = (active * up_pre).astype(jnp.bfloat16)
    d_hidden = jnp.einsum("scd,hd->sch", grad_rows, down_rows, preferred_element_type=jnp.float32)
    d_gate = (d_hidden * up_pre * gate_sig * (1.0 + gate_pre * (1.0 - gate_sig))).astype(
        jnp.bfloat16
    )
    d_up = (d_hidden * active).astype(jnp.bfloat16)
    d_rows = jnp.einsum("sch,dh->scd", d_gate, gate_cols, preferred_element_type=jnp.float32)
    d_rows = (
        d_rows + jnp.einsum("sch,dh->scd", d_up, up_cols, preferred_element_type=jnp.float32)
    ).astype(jnp.bfloat16)
    terms = jnp.sum(hidden.astype(jnp.float32) * d_hidden, axis=2).astype(jnp.bfloat16)
    return (d_rows, terms)


def local(
    fwd_act, fwd_route, fwd_weight, bwd_act, bwd_grad, bwd_route, bwd_weight, w_gate, w_up, w_down
):
    layer_in = passed_along(fwd_act, "section", 1)[0]
    grad_in = passed_along(bwd_grad, "section", -1)[0]
    gate_cols = w_gate[0]
    up_cols = w_up[0]
    down_rows = w_down[0]
    group_size = FF // gate_cols.shape[1]
    experts = lax.axis_size("expert") // group_size
    tok_count = layer_in.shape[0]
    capacity = 3 * tok_count // (4 * experts)
    select_f, place_f, inside_f = route_plan(fwd_route[0], experts, capacity)
    select_b, place_b, inside_b = route_plan(bwd_route[0], experts, capacity)
    sent_f = pack_rows(select_f, layer_in, group_size)
    sent_x = pack_rows(select_b, bwd_act[0], group_size)
    sent_g = pack_rows(select_b, grad_in, group_size)
    part_out = expert_forward(
        lax.all_to_all(sent_f, "expert", split_axis=0, concat_axis=0, tiled=True),
        gate_cols,
        up_cols,
        down_rows,
    )
    back_f = lax.all_to_all(part_out, "expert", split_axis=0, concat_axis=0, tiled=True)
    d_rows, terms = expert_backward(
        lax.all_to_all(sent_x, "expert", split_axis=0, concat_axis=0, tiled=True),
        lax.all_to_all(sent_g, "expert", split_axis=0, concat_axis=0, tiled=True),
        gate_cols,
        up_cols,
        down_rows,
    )
    back_x = lax.all_to_all(d_rows, "expert", split_axis=0, concat_axis=0, tiled=True)
    back_w = lax.all_to_all(terms, "expert", split_axis=0, concat_axis=0, tiled=True)
    total_f = unpack_sum(back_f, group_size, place_f, inside_f)
    total_x = unpack_sum(back_x, group_size, place_b, inside_b)
    gate_grad = unpack_sum(back_w, group_size, place_b, inside_b)
    mixed = (layer_in.astype(jnp.float32) + fwd_weight[0][:, None] * total_f).astype(jnp.bfloat16)
    input_grad = (grad_in.astype(jnp.float32) + bwd_weight[0][:, None] * total_x).astype(
        jnp.bfloat16
    )
    return (mixed[None], input_grad[None], gate_grad[None])


def solution(mesh):
    placed = (
        P("section", "expert", None),
        P("section", "expert"),
        P("section", "expert"),
        P("section", "expert", None),
        P("section", "expert", None),
        P("section", "expert"),
        P("section", "expert"),
        P("section", None, "expert"),
        P("section", None, "expert"),
        P("section", "expert", None),
    )
    return jax.shard_map(
        local,
        mesh=mesh,
        in_specs=placed,
        out_specs=(
            P("section", "expert", None),
            P("section", "expert", None),
            P("section", "expert"),
        ),
        check_vma=False,
    )
```

profile of v0, /device:TPU:13, one launch (start us, length us, event | category | flops | bytes accessed | tf_op | source)
XLA Modules:
  0.0 362.3 jit_solution(12279977348761897054)
XLA Ops:
  3.1 1.2 convolution_convert_fusion.1
  4.3 1.8 broadcast_in_dim.65
  6.1 6.7 %all-to-all-start.3 = ((bf16[16,24,3584]{2,1,0:T(8,128)(2,1)}), bf16[16,24,3584]{2,1,0:T(8,128)(2,1)}, u32[]{:S(2)}, u32[]{:S(2)}) async-start(bf16[16,24,3584]{2,1,0:T(8,128)(2,1)} %bitcast.123), calls=%async_computation.3 | async-start | bytes 5505024 | tf_op jit(solution)/shard_map/all_to_all | solution.py:103
  12.8 1.3 collective-permute-start.1
  14.0 10.6 %collective-permute-done.1 = bf16[1,64,3584]{2,1,0:T(8,128)(2,1)S(1)} collective-permute-done((bf16[1,64,3584]{2,1,0:T(8,128)(2,1)S(1)}, bf16[1,64,3584]{2,1,0:T(8,128)(2,1)S(1)}, u32[]{:S(2)}, u32[]{:S(2)}) %collective-permute-start.1) | collective-permute-done | bytes 458784 | tf_op jit(solution)/shard_map/ppermute | solution.py:12
  25.7 48.6 %all-to-all-done.3 = bf16[16,24,3584]{2,1,0:T(8,128)(2,1)} async-done(((bf16[16,24,3584]{2,1,0:T(8,128)(2,1)}), bf16[16,24,3584]{2,1,0:T(8,128)(2,1)}, u32[]{:S(2)}, u32[]{:S(2)}) %all-to-all-start.3) | async-done | bytes 2752544 | tf_op jit(solution)/shard_map/all_to_all | solution.py:103
  74.3 1.7 broadcast_in_dim.64
  76.1 5.0 %all-to-all-start.2 = ((bf16[16,24,3584]{2,1,0:T(8,128)(2,1)}), bf16[16,24,3584]{2,1,0:T(8,128)(2,1)}, u32[]{:S(2)}, u32[]{:S(2)}) async-start(bf16[16,24,3584]{2,1,0:T(8,128)(2,1)} %bitcast.121), calls=%async_computation.2 | async-start | bytes 5505024 | tf_op jit(solution)/shard_map/all_to_all | solution.py:104
  81.1 1.3 collective-permute-start
  82.8 10.3 %collective-permute-done = bf16[1,64,3584]{2,1,0:T(8,128)(2,1)S(1)} collective-permute-done((bf16[1,64,3584]{2,1,0:T(8,128)(2,1)S(1)}, bf16[1,64,3584]{2,1,0:T(8,128)(2,1)S(1)}, u32[]{:S(2)}, u32[]{:S(2)}) %collective-permute-start) | collective-permute-done | bytes 458784 | tf_op jit(solution)/shard_map/ppermute | solution.py:12
  93.3 49.4 %all-to-all-done.2 = bf16[16,24,3584]{2,1,0:T(8,128)(2,1)} async-done(((bf16[16,24,3584]{2,1,0:T(8,128)(2,1)}), bf16[16,24,3584]{2,1,0:T(8,128)(2,1)}, u32[]{:S(2)}, u32[]{:S(2)}) %all-to-all-start.2) | async-done | bytes 2752544 | tf_op jit(solution)/shard_map/all_to_all | solution.py:104
  142.7 1.8 broadcast_in_dim.33
  144.5 5.0 %all-to-all-start = ((bf16[16,24,3584]{2,1,0:T(8,128)(2,1)}), bf16[16,24,3584]{2,1,0:T(8,128)(2,1)}, u32[]{:S(2)}, u32[]{:S(2)}) async-start(bf16[16,24,3584]{2,1,0:T(8,128)(2,1)} %bitcast.122), calls=%async_computation | async-start | bytes 5505024 | tf_op jit(solution)/shard_map/all_to_all | solution.py:96
  149.5 2.7 fusion.18
  152.2 2.7 fusion.12
  155.0 2.7 multiply_reduce_fusion
  158.3 3.3 fusion.16
  161.6 49.5 %all-to-all-done = bf16[16,24,3584]{2,1,0:T(8,128)(2,1)} async-done(((bf16[16,24,3584]{2,1,0:T(8,128)(2,1)}), bf16[16,24,3584]{2,1,0:T(8,128)(2,1)}, u32[]{:S(2)}, u32[]{:S(2)}) %all-to-all-start) | async-done | bytes 2752544 | tf_op jit(solution)/shard_map/all_to_all | solution.py:96
  211.1 4.9 %all-to-all-start.5 = ((bf16[16,1,24]{2,1,0:T(2,128)(2,1)}), bf16[16,1,24]{2,1,0:T(2,128)(2,1)S(1)}, u32[]{:S(2)}, u32[]{:S(2)}) async-start(bf16[16,1,24]{2,1,0:T(2,128)(2,1)} %copy.13), calls=%async_computation.5 | async-start | bytes 16384 | tf_op jit(solution)/shard_map/all_to_all | solution.py:110
  216.0 5.1 %fusion = bf16[16,24,3584]{2,1,0:T(8,128)(2,1)} fusion(f32[16,24,3584]{2,1,0:T(8,128)} %fusion.16, bf16[1,3584,128]{2,1,0:T(8,128)(2,1)S(1)} %copy-done, f32[16,24,128]{2,1,0:T(8,128)S(1)} %get-tuple-element.4, f32[16,24,128]{2,1,0:T(8,128)S(1)} %fusion.18), kind=kOutput, calls=%fused_computation.4 | convolution fusion | flops 355368960 | bytes 9568256 | tf_op jit(solution)/shard_map/sch,dh->scd/dot_general | solution.py:72
  221.1 6.0 %all-to-all-start.4 = ((bf16[16,24,3584]{2,1,0:T(8,128)(2,1)}), bf16[16,24,3584]{2,1,0:T(8,128)(2,1)}, u32[]{:S(2)}, u32[]{:S(2)}) async-start(bf16[16,24,3584]{2,1,0:T(8,128)(2,1)} %fusion), calls=%async_computation.4 | async-start | bytes 5505024 | tf_op jit(solution)/shard_map/all_to_all | solution.py:109
  227.1 2.7 fusion.20
  229.8 6.5 %convolution_convert_fusion = bf16[16,24,3584]{2,1,0:T(8,128)(2,1)} fusion(bf16[16,24,3584]{2,1,0:T(8,128)(2,1)} %all-to-all-done, bf16[1,128,3584]{2,1,0:T(8,128)(2,1)S(1)} %copy-done.4, bf16[1,3584,128]{2,1,0:T(8,128)(2,1)S(1)} %copy-done, f32[16,24,128]{2,1,0:T(8,128)S(1)} %fusion.20), kind=kOutput, calls=%fused_computation.5 | convolution fusion | flops 706314240 | bytes 7536640 | tf_op jit(solution)/shard_map/sch,hd->scd/dot_general | solution.py:54
  236.3 52.4 %all-to-all-done.4 = bf16[16,24,3584]{2,1,0:T(8,128)(2,1)} async-done(((bf16[16,24,3584]{2,1,0:T(8,128)(2,1)}), bf16[16,24,3584]{2,1,0:T(8,128)(2,1)}, u32[]{:S(2)}, u32[]{:S(2)}) %all-to-all-start.4) | async-done | bytes 2752544 | tf_op jit(solution)/shard_map/all_to_all | solution.py:109
  288.7 4.9 %all-to-all-start.1 = ((bf16[16,24,3584]{2,1,0:T(8,128)(2,1)}), bf16[16,24,3584]{2,1,0:T(8,128)(2,1)}, u32[]{:S(2)}, u32[]{:S(2)}) async-start(bf16[16,24,3584]{2,1,0:T(8,128)(2,1)} %convolution_convert_fusion), calls=%async_computation.1 | async-start | bytes 5505024 | tf_op jit(solution)/shard_map/all_to_all | solution.py:101
  295.1 2.2 convert_reduce_fusion
  297.3 0.9 gather_fusion.1
  298.2 57.0 %all-to-all-done.1 = bf16[16,24,3584]{2,1,0:T(8,128)(2,1)} async-done(((bf16[16,24,3584]{2,1,0:T(8,128)(2,1)}), bf16[16,24,3584]{2,1,0:T(8,128)(2,1)}, u32[]{:S(2)}, u32[]{:S(2)}) %all-to-all-start.1) | async-done | bytes 2752544 | tf_op jit(solution)/shard_map/all_to_all | solution.py:101
  355.2 2.2 convert_reduce_fusion.1
  357.4 0.9 gather_fusion
  358.3 2.0 fusion.4
  360.3 2.0 fusion.7
  (47 shorter events, 6.1 us)
Async XLA Ops:
  0.6 151.6 %copy-start = (bf16[1,3584,128]{2,1,0:T(8,128)(2,1)S(1)}, bf16[1,3584,128]{2,1,0:T(8,128)(2,1)}, u32[]{:S(2)}) copy-start(bf16[1,3584,128]{2,1,0:T(8,128)(2,1)} %param.18) | copy-start | bytes 2752516
  6.1 6.7 %copy-start.9 = (bf16[1,64,3584]{2,1,0:T(8,128)(2,1)S(1)}, bf16[1,64,3584]{2,1,0:T(8,128)(2,1)}, u32[]{:S(2)}) copy-start(bf16[1,64,3584]{2,1,0:T(8,128)(2,1)} %param.14) | copy-start | bytes 1376260
  6.1 68.3 %all-to-all-start.3 = ((bf16[16,24,3584]{2,1,0:T(8,128)(2,1)}), bf16[16,24,3584]{2,1,0:T(8,128)(2,1)}, u32[]{:S(2)}, u32[]{:S(2)}) async-start(bf16[16,24,3584]{2,1,0:T(8,128)(2,1)} %bitcast.123), calls=%async_computation.3 | async-start | bytes 5505024 | tf_op jit(solution)/shard_map/all_to_all | solution.py:103
  12.8 11.9 %collective-permute-start.1 = (bf16[1,64,3584]{2,1,0:T(8,128)(2,1)S(1)}, bf16[1,64,3584]{2,1,0:T(8,128)(2,1)S(1)}, u32[]{:S(2)}, u32[]{:S(2)}) collective-permute-start(bf16[1,64,3584]{2,1,0:T(8,128)(2,1)S(1)} %copy-done.9), channel_id=1, source_target_pairs={{16,0},{0,16},{17,1},{1,17},{18,2},{2,18},{19,3},{3,19},{20,4},{4,... | collective-permute-start | bytes 1376264 | tf_op jit(solution)/shard_map/ppermute | solution.py:12
  24.7 0.8 copy-start.2
  76.1 5.0 %copy-start.10 = (bf16[1,64,3584]{2,1,0:T(8,128)(2,1)S(1)}, bf16[1,64,3584]{2,1,0:T(8,128)(2,1)}, u32[]{:S(2)}) copy-start(bf16[1,64,3584]{2,1,0:T(8,128)(2,1)} %param.10) | copy-start | bytes 1376260
  76.1 6.3 %copy-start.5 = (s32[1,64]{1,0:T(1,128)S(1)}, s32[1,64]{1,0:T(1,128)}, u32[]{:S(2)}) copy-start(s32[1,64]{1,0:T(1,128)} %param.11) | copy-start | bytes 772
  76.1 66.6 %all-to-all-start.2 = ((bf16[16,24,3584]{2,1,0:T(8,128)(2,1)}), bf16[16,24,3584]{2,1,0:T(8,128)(2,1)}, u32[]{:S(2)}, u32[]{:S(2)}) async-start(bf16[16,24,3584]{2,1,0:T(8,128)(2,1)} %bitcast.121), calls=%async_computation.2 | async-start | bytes 5505024 | tf_op jit(solution)/shard_map/all_to_all | solution.py:104
  81.1 11.9 %collective-permute-start = (bf16[1,64,3584]{2,1,0:T(8,128)(2,1)S(1)}, bf16[1,64,3584]{2,1,0:T(8,128)(2,1)S(1)}, u32[]{:S(2)}, u32[]{:S(2)}) collective-permute-start(bf16[1,64,3584]{2,1,0:T(8,128)(2,1)S(1)} %copy-done.10), channel_id=1, source_target_pairs={{16,0},{0,16},{17,1},{1,17},{18,2},{2,18},{19,3},{3,19},{20,4},{4,... | collective-permute-start | bytes 1376264 | tf_op jit(solution)/shard_map/ppermute | solution.py:12
  93.0 51.5 %copy-start.3 = (bf16[1,64,3584]{2,1,0:T(8,128)(2,1)}, bf16[1,64,3584]{2,1,0:T(8,128)(2,1)S(1)}, u32[]{:S(2)}) copy-start(bf16[1,64,3584]{2,1,0:T(8,128)(2,1)S(1)} %collective-permute-done) | copy-start | bytes 1376260
  144.5 5.0 %copy-start.1 = (bf16[1,3584,128]{2,1,0:T(8,128)(2,1)S(1)}, bf16[1,3584,128]{2,1,0:T(8,128)(2,1)}, u32[]{:S(2)}) copy-start(bf16[1,3584,128]{2,1,0:T(8,128)(2,1)} %param.17) | copy-start | bytes 2752516
  144.5 66.6 %all-to-all-start = ((bf16[16,24,3584]{2,1,0:T(8,128)(2,1)}), bf16[16,24,3584]{2,1,0:T(8,128)(2,1)}, u32[]{:S(2)}, u32[]{:S(2)}) async-start(bf16[16,24,3584]{2,1,0:T(8,128)(2,1)} %bitcast.122), calls=%async_computation | async-start | bytes 5505024 | tf_op jit(solution)/shard_map/all_to_all | solution.py:96
  152.2 2.8 copy-start.4
  211.1 10.0 %all-to-all-start.5 = ((bf16[16,1,24]{2,1,0:T(2,128)(2,1)}), bf16[16,1,24]{2,1,0:T(2,128)(2,1)S(1)}, u32[]{:S(2)}, u32[]{:S(2)}) async-start(bf16[16,1,24]{2,1,0:T(2,128)(2,1)} %copy.13), calls=%async_computation.5 | async-start | bytes 16384 | tf_op jit(solution)/shard_map/all_to_all | solution.py:110
  221.1 67.6 %all-to-all-start.4 = ((bf16[16,24,3584]{2,1,0:T(8,128)(2,1)}), bf16[16,24,3584]{2,1,0:T(8,128)(2,1)}, u32[]{:S(2)}, u32[]{:S(2)}) async-start(bf16[16,24,3584]{2,1,0:T(8,128)(2,1)} %fusion), calls=%async_computation.4 | async-start | bytes 5505024 | tf_op jit(solution)/shard_map/all_to_all | solution.py:109
  236.3 57.3 %copy-start.6 = (s32[1,64]{1,0:T(1,128)S(1)}, s32[1,64]{1,0:T(1,128)}, u32[]{:S(2)}) copy-start(s32[1,64]{1,0:T(1,128)} %param.15) | copy-start | bytes 772
  288.7 66.5 %all-to-all-start.1 = ((bf16[16,24,3584]{2,1,0:T(8,128)(2,1)}), bf16[16,24,3584]{2,1,0:T(8,128)(2,1)}, u32[]{:S(2)}, u32[]{:S(2)}) async-start(bf16[16,24,3584]{2,1,0:T(8,128)(2,1)} %convolution_convert_fusion), calls=%async_computation.1 | async-start | bytes 5505024 | tf_op jit(solution)/shard_map/all_to_all | solution.py:101
  357.4 0.9 copy-start.7
  357.4 2.9 copy-start.8
where the time goes:
time: 363 us; the launch traced here: 362 us
  waiting for transfers between devices  278 us (77%)
  starting transfers between devices  35.2 us (10%)
  matrix products  27.4 us (8%)
  other arithmetic  11.8 us (3%)
  local copies, waits for them, and re-layouts  9.35 us (3%)
    all_to_all x1, waiting for transfers between devices, local(): lax.all_to_all(part_out, 'expert', split_axis=0, concat_axis=0, tiled=True)  57 us
    all_to_all x1, waiting for transfers between devices, local(): lax.all_to_all(d_rows, 'expert', split_axis=0, concat_axis=0, tiled=True)  52.4 us
    all_to_all x1, waiting for transfers between devices, local(): lax.all_to_all(sent_f, 'expert', split_axis=0, concat_axis=0, tiled=True)  49.5 us
    all_to_all x1, waiting for transfers between devices, local(): lax.all_to_all(sent_g, 'expert', split_axis=0, concat_axis=0, tiled=True)  49.4 us
    all_to_all x1, waiting for transfers between devices, local(): lax.all_to_all(sent_x, 'expert', split_axis=0, concat_axis=0, tiled=True)  48.6 us
    ppermute x2, waiting for transfers between devices, passed_along(): return lax.ppermute(block, axis, route)  20.9 us
  transfers between devices with their start and end apart: 8, of which 7 were waited for; matrix products, arithmetic and copies ran while one was open for 9% of the time, Pallas kernels for 0%

commit v1 on v0

--- a/solution.py
+++ b/solution.py
@@ -1,6 +1,10 @@
+import functools
+
 import jax
 import jax.numpy as jnp
 from jax import lax
+from jax.experimental import pallas as pl
+from jax.experimental.pallas import tpu as pltpu
 from jax.sharding import PartitionSpec as P
 
 FF = 1024
@@ -118,6 +122,426 @@
     return (mixed[None], input_grad[None], gate_grad[None])
 
 
+MESH = pl.DeviceIdType.MESH
+X, F, G = 0, 1, 2
+STEP = 512
+HALF_STEP = 256
+
+
+def flip(index, bit):
+    return index + bit - 2 * bit * lax.rem(lax.div(index, bit), 2)
+
+
+def make_plan(route_row, own_expert, capacity):
+    count = route_row.shape[1]
+    row = route_row.astype(jnp.float32)
+    at_row = lax.broadcasted_iota(jnp.int32, (count, count), 0)
+    at_col = lax.broadcasted_iota(jnp.int32, (count, count), 1)
+    wide = jnp.broadcast_to(row, (count, count))
+    col = jnp.sum(jnp.where(at_row == at_col, wide, 0.0), axis=1, keepdims=True)
+    same = jnp.where(wide == col, 1.0, 0.0)
+    slot_col = jnp.sum(jnp.where(at_col < at_row, same, 0.0), axis=1, keepdims=True)
+    slot_row = jnp.sum(jnp.where(at_row < at_col, same, 0.0), axis=0, keepdims=True)
+    own = own_expert.astype(jnp.float32)
+
+    def onehot(shape, axis, route, slot):
+        at = lax.broadcasted_iota(jnp.int32, shape, axis).astype(jnp.float32)
+        first = at < capacity
+        expert = jnp.where(first, own, 1.0 - own)
+        place = jnp.where(first, at, at - capacity)
+        hit = jnp.where(route == expert, 1.0, 0.0) * jnp.where(slot == place, 1.0, 0.0)
+        return hit.astype(jnp.bfloat16)
+
+    pick = onehot((2 * capacity, count), 0, row, slot_row)
+    spread = onehot((count, 2 * capacity), 1, col, slot_col)
+    return pick, spread
+
+
+def as_column(row):
+    count = row.shape[1]
+    at_row = lax.broadcasted_iota(jnp.int32, (count, count), 0)
+    at_col = lax.broadcasted_iota(jnp.int32, (count, count), 1)
+    wide = jnp.broadcast_to(row, (count, count))
+    return jnp.sum(jnp.where(at_row == at_col, wide, 0.0), axis=1, keepdims=True)
+
+
+def as_row(col):
+    count = col.shape[0]
+    at_row = lax.broadcasted_iota(jnp.int32, (count, count), 0)
+    at_col = lax.broadcasted_iota(jnp.int32, (count, count), 1)
+    wide = jnp.broadcast_to(col, (count, count))
+    return jnp.sum(jnp.where(at_row == at_col, wide, 0.0), axis=0, keepdims=True)
+
+
+def dot(a, b):
+    return jnp.dot(a, b, preferred_element_type=jnp.float32)
+
+
+def dot_t(a, b):
+    return lax.dot_general(a, b, (((1,), (1,)), ((), ())), preferred_element_type=jnp.float32)
+
+
+def layer_kernel(
+    capacity,
+    fa, fr, fw, ba, bg, br, bw, wg_hbm, wu_hbm, wd_hbm,
+    mixed, in_grad, gate_grad,
+    xf, xg, fold_s, fold_r, rows, wgu, wd, pre_x, pre_f, d_hid, hid, dd,
+    part_f, part_x, core_f, core_x, two_f, two_x, one_f, one_x, last_s, last_r, own_s,
+    w_sem, relay_s, relay_r, mir_s, mir_r, row_s, row_r, c_s, c_r, t_s, t_r, o_s, o_r, l_s, l_r,
+):
+    depth = fa.shape[1]
+    half = depth // 2
+    total = rows.shape[1] * rows.shape[2]
+    unit = wd.shape[0]
+    cap = capacity
+    section = lax.axis_index("section")
+    me = lax.axis_index("expert")
+    core = lax.rem(me, 2)
+    j = lax.rem(me, 8)
+    base = me - j
+    across, along = flip(j, 4), flip(j, 2)
+    p1 = (1 - core) * across + core * along
+    p2 = (1 - core) * along + core * across
+    p12 = flip(flip(j, 4), 2)
+    other = flip(j, 1)
+
+    def in_group(k):
+        return (section, base + k)
+
+    mirror = (section, flip(me, 8))
+    relay = (1 - section, me)
+    barrier = pltpu.get_barrier_semaphore()
+    for target in (relay, mirror, in_group(p1), in_group(p2), in_group(other)):
+        pl.semaphore_signal(barrier, inc=1, device_id=target, device_id_type=MESH)
+    pl.semaphore_wait(barrier, 5)
+
+    def remote(src, dst, send, recv, target):
+        return pltpu.make_async_remote_copy(
+            src_ref=src, dst_ref=dst, send_sem=send, recv_sem=recv,
+            device_id=target, device_id_type=MESH,
+        )
+
+    sent = []
+
+    def go(copy):
+        copy.start()
+        sent.append(copy)
+        return copy
+
+    relay_f = remote(fa, xf, relay_s.at[0], relay_r.at[0], relay)
+    relay_g = remote(bg, xg, relay_s.at[1], relay_r.at[1], relay)
+    relay_f.start()
+    loads = [
+        pltpu.make_async_copy(wg_hbm, wgu.at[:, pl.ds(0, unit)], w_sem.at[0]),
+        pltpu.make_async_copy(wu_hbm, wgu.at[:, pl.ds(unit, unit)], w_sem.at[1]),
+        pltpu.make_async_copy(wd_hbm, wd, w_sem.at[2]),
+    ]
+    for load in loads:
+        load.start()
+    own_expert = lax.div(me, 8)
+    pick_b, spread_b = make_plan(br[...], own_expert, cap)
+    pick_f, spread_f = make_plan(fr[...], own_expert, cap)
+    picks = (pick_b, pick_f, pick_b)
+    sources = (ba, xf, xg)
+
+    def halves(k):
+        lo = pl.ds(pl.multiple_of(k * HALF_STEP, HALF_STEP), HALF_STEP)
+        hi = pl.ds(pl.multiple_of(half + k * HALF_STEP, HALF_STEP), HALF_STEP)
+        return lo, hi
+
+    def mirror_copy(t):
+        return remote(fold_s.at[t], fold_r.at[t], mir_s.at[t], mir_r.at[t], mirror)
+
+    def pack(t):
+        @pl.loop(0, half // HALF_STEP)
+        def _(k):
+            lo, hi = halves(k)
+            away = picks[t][cap:]
+            left, right = dot(away, sources[t][:, lo]), dot(away, sources[t][:, hi])
+            fold_s[t, :, lo] = jnp.concatenate([left, right], axis=0).astype(jnp.bfloat16)
+
+        go(mirror_copy(t))
+
+    def row_copy(t, slot, send_at, target):
+        block = rows.at[t, slot]
+        return remote(block, block, row_s.at[t, send_at], row_r.at[t, slot], in_group(target))
+
+    def form(t):
+        mirror_copy(t).wait_recv()
+
+        @pl.loop(0, half // HALF_STEP)
+        def _(k):
+            lo, hi = halves(k)
+            near = picks[t][:cap]
+            left, right = dot(near, sources[t][:, lo]), dot(near, sources[t][:, hi])
+            got = fold_r[t, :, lo].astype(jnp.float32)
+            rows[t, j, :, lo] = jnp.concatenate([left, got[:cap]], axis=0).astype(jnp.bfloat16)
+            rows[t, j, :, hi] = jnp.concatenate([right, got[cap:]], axis=0).astype(jnp.bfloat16)
+
+        go(row_copy(t, j, 0, p1))
+        go(row_copy(t, j, 1, p2))
+        go(row_copy(t, j, 2, other))
+
+    def forward_first(t):
+        row_copy(t, p1, 3, p2).wait_recv()
+        go(row_copy(t, p1, 3, p2))
+        go(row_copy(t, p1, 4, other))
+
+    def forward_second(t):
+        row_copy(t, p2, 5, other).wait_recv()
+        go(row_copy(t, p2, 5, other))
+        row_copy(t, p12, 6, other).wait_recv()
+        go(row_copy(t, p12, 6, other))
+
+    def gathered(t):
+        for k in range(4):
+            row_copy(t, 2 * k + 1 - core, 0, other).wait_recv()
+
+    def columns(k):
+        return pl.ds(pl.multiple_of(k * STEP, STEP), STEP)
+
+    def gate_up(t, out):
+        out[...] = jnp.zeros_like(out)
+
+        @pl.loop(0, depth // STEP)
+        def _(k):
+            cols = columns(k)
+            out[...] += dot(rows[t, :, :, cols].reshape(total, STEP), wgu[cols, :])
+
+    def core_copy(o, k):
+        part, box = ((part_f, core_f), (part_x, core_x))[o]
+        return remote(
+            part.at[2 * k + 1 - core], box.at[k], c_s.at[o, k], c_r.at[o, k], in_group(other)
+        )
+
+    def two_copy(o, k):
+        part, box = ((part_f, two_f), (part_x, two_x))[o]
+        return remote(
+            part.at[(p2, p12)[k]], box.at[k], t_s.at[o, k], t_r.at[o, k], in_group(p2)
+        )
+
+    def one_copy(o):
+        part, box = ((part_f, one_f), (part_x, one_x))[o]
+        return remote(part.at[p1], box, o_s.at[o], o_r.at[o], in_group(p1))
+
+    def last_copy(o):
+        return remote(last_s.at[o], last_r.at[o], l_s.at[o], l_r.at[o], mirror)
+
+    def add_into(ref, slot, box):
+        ref[slot] = (
+            ref[slot].astype(jnp.float32) + box.astype(jnp.float32)
+        ).astype(jnp.bfloat16)
+
+    def merge_core(o):
+        part, box = ((part_f, core_f), (part_x, core_x))[o]
+        for k in range(4):
+            core_copy(o, k).wait_recv()
+
+        @pl.loop(0, 4)
+        def _(k):
+            add_into(part, 2 * k + core, box[k])
+
+        go(two_copy(o, 0))
+        go(two_copy(o, 1))
+
+    def merge_two(o):
+        part, box = ((part_f, two_f), (part_x, two_x))[o]
+        two_copy(o, 1).wait_recv()
+        add_into(part, p1, box[1])
+        go(one_copy(o))
+        two_copy(o, 0).wait_recv()
+        add_into(part, j, box[0])
+
+    def merge_one(o):
+        part, box = ((part_f, one_f), (part_x, one_x))[o]
+        one_copy(o).wait_recv()
+
+        def both(cols):
+            return part[j, :, cols].astype(jnp.float32) + box[:, cols].astype(jnp.float32)
+
+        @pl.loop(0, half // HALF_STEP)
+        def _(k):
+            lo, hi = halves(k)
+            left, right = both(lo), both(hi)
+            own_s[o, :, lo] = left[:cap]
+            own_s[o, :, hi] = right[:cap]
+            last_s[o, :, lo] = jnp.concatenate([left[cap:], right[cap:]], axis=0).astype(
+                jnp.bfloat16
+            )
+
+        if o == 1:
+            tail = both(pl.ds(depth, 128))
+            own_s[o, :, pl.ds(depth, 128)] = tail[:cap]
+            last_s[o, :, pl.ds(half, 128)] = jnp.concatenate(
+                [tail[cap:], tail[cap:]], axis=0
+            ).astype(jnp.bfloat16)
+        else:
+            last_s[o, :, pl.ds(half, 128)] = jnp.zeros((2 * cap, 128), jnp.bfloat16)
+        go(last_copy(o))
+
+    def finish(o, spread, weight_row, base_rows, out):
+        last_copy(o).wait_recv()
+        weight = as_column(weight_row)
+
+        def spread_sum(near, far):
+            return dot(spread, jnp.concatenate([near, far], axis=0).astype(jnp.bfloat16))
+
+        @pl.loop(0, half // HALF_STEP)
+        def _(k):
+            lo, hi = halves(k)
+            got = last_r[o, :, lo].astype(jnp.float32)
+            for cols, far in ((lo, got[:cap]), (hi, got[cap:])):
+                value = spread_sum(own_s[o, :, cols], far)
+                out[:, cols] = (
+                    base_rows[:, cols].astype(jnp.float32) + weight * value
+                ).astype(jnp.bfloat16)
+
+        if o == 1:
+            far = last_r[o, :, pl.ds(half, 128)].astype(jnp.float32)[:cap]
+            value = spread_sum(own_s[o, :, pl.ds(depth, 128)], far)
+            gate_grad[...] = as_row(value[:, :1])
+
+    pack(X)
+    relay_f.wait_send()
+    relay_g.start()
+    form(X)
+    relay_f.wait_recv()
+    pack(F)
+    forward_first(X)
+    form(F)
+    forward_second(X)
+    relay_g.wait_recv()
+    pack(G)
+    forward_first(F)
+    for load in loads:
+        load.wait()
+    gathered(X)
+    gate_up(X, pre_x)
+    form(G)
+    forward_second(F)
+    forward_first(G)
+    gathered(F)
+    gate_up(F, pre_f)
+    gate = pre_f[:, :unit]
+    hid[...] = (gate * jax.nn.sigmoid(gate) * pre_f[:, unit:]).astype(jnp.bfloat16)
+
+    @pl.loop(0, depth // STEP)
+    def _(k):
+        cols = columns(k)
+        part_f[:, :, cols] = (
+            dot(hid[...], wd[:, cols]).astype(jnp.bfloat16).reshape(8, 2 * cap, STEP)
+        )
+
+    for k in range(4):
+        go(core_copy(0, k))
+    forward_second(G)
+    merge_core(0)
+    gathered(G)
+    d_hid[...] = jnp.zeros_like(d_hid)
+
+    @pl.loop(0, depth // STEP)
+    def _(k):
+        cols = columns(k)
+        d_hid[...] += dot_t(rows[G, :, :, cols].reshape(total, STEP), wd[:, cols])
+
+    gate = pre_x[:, :unit]
+    up = pre_x[:, unit:]
+    sig = jax.nn.sigmoid(gate)
+    active = gate * sig
+    hidden = (active * up).astype(jnp.bfloat16).astype(jnp.float32)
+    grad = d_hid[...]
+    dd[:, :unit] = (grad * up * sig * (1.0 + gate * (1.0 - sig))).astype(jnp.bfloat16)
+    dd[:, unit:] = (grad * active).astype(jnp.bfloat16)
+    term = jnp.sum(hidden * grad, axis=1, keepdims=True)
+    part_x[:, :, pl.ds(depth, 128)] = (
+        jnp.broadcast_to(term, (total, 128)).astype(jnp.bfloat16).reshape(8, 2 * cap, 128)
+    )
+
+    @pl.loop(0, depth // STEP)
+    def _(k):
+        cols = columns(k)
+        part_x[:, :, cols] = (
+            dot_t(dd[...], wgu[cols, :]).astype(jnp.bfloat16).reshape(8, 2 * cap, STEP)
+        )
+
+    for k in range(4):
+        go(core_copy(1, k))
+    merge_two(0)
+    merge_core(1)
+    merge_one(0)
+    merge_two(1)
+    finish(0, spread_f, fw[...], xf, mixed)
+    merge_one(1)
+    finish(1, spread_b, bw[...], xg, in_grad)
+    relay_g.wait_send()
+    for copy in sent:
+        copy.wait_send()
+
+
+def local_tree(
+    fwd_act, fwd_route, fwd_weight, bwd_act, bwd_grad, bwd_route, bwd_weight, w_gate, w_up, w_down
+):
+    count, depth = fwd_act.shape[1:]
+    unit = w_gate.shape[2]
+    cap = 3 * count // 8
+    pair = 2 * cap
+    wide = depth + 128
+    half = depth // 2
+    bf16, f32 = jnp.bfloat16, jnp.float32
+    vmem = pl.BlockSpec(memory_space=pltpu.VMEM)
+    hbm = pl.BlockSpec(memory_space=pl.ANY)
+    dma = pltpu.SemaphoreType.DMA
+    buf = pltpu.VMEM
+    mixed, in_grad, gate_grad = pl.pallas_call(
+        functools.partial(layer_kernel, cap),
+        out_shape=(
+            jax.ShapeDtypeStruct((count, depth), bf16),
+            jax.ShapeDtypeStruct((count, depth), bf16),
+            jax.ShapeDtypeStruct((1, count), f32),
+        ),
+        in_specs=[vmem] * 7 + [hbm] * 3,
+        out_specs=(vmem, vmem, vmem),
+        scratch_shapes=[
+            buf((count, depth), bf16),
+            buf((count, depth), bf16),
+            buf((3, pair, half), bf16),
+            buf((3, pair, half), bf16),
+            buf((3, 8, pair, depth), bf16),
+            buf((depth, 2 * unit), bf16),
+            buf((unit, depth), bf16),
+            buf((8 * pair, 2 * unit), f32),
+            buf((8 * pair, 2 * unit), f32),
+            buf((8 * pair, unit), f32),
+            buf((8 * pair, unit), bf16),
+            buf((8 * pair, 2 * unit), bf16),
+            buf((8, pair, depth), bf16),
+            buf((8, pair, wide), bf16),
+            buf((4, pair, depth), bf16),
+            buf((4, pair, wide), bf16),
+            buf((2, pair, depth), bf16),
+            buf((2, pair, wide), bf16),
+            buf((pair, depth), bf16),
+            buf((pair, wide), bf16),
+            buf((2, pair, half + 128), bf16),
+            buf((2, pair, half + 128), bf16),
+            buf((2, cap, wide), f32),
+            dma((3,)), dma((2,)), dma((2,)), dma((3,)), dma((3,)),
+            dma((3, 7)), dma((3, 8)), dma((2, 4)), dma((2, 4)), dma((2, 2)), dma((2, 2)),
+            dma((2,)), dma((2,)), dma((2,)), dma((2,)),
+        ],
+        compiler_params=pltpu.CompilerParams(
+            collective_id=0, has_side_effects=True, vmem_limit_bytes=50 * 1024 * 1024
+        ),
+        cost_estimate=pl.CostEstimate(
+            flops=2 * 8 * 8 * pair * depth * unit, bytes_accessed=6_000_000, transcendentals=100_000
+        ),
+    )(
+        fwd_act[0], fwd_route, fwd_weight, bwd_act[0], bwd_grad[0], bwd_route, bwd_weight,
+        w_gate[0], w_up[0], w_down[0],
+    )
+    return (mixed[None], in_grad[None], gate_grad)
+
+
 def solution(mesh):
     placed = (
         P("section", "expert", None),
@@ -131,8 +555,9 @@
         P("section", None, "expert"),
         P("section", "expert", None),
     )
+    pair_of_experts = mesh.shape["section"] == 2 and mesh.shape["expert"] == 16
     return jax.shard_map(
-        local,
+        local_tree if pair_of_experts else local,
         mesh=mesh,
         in_specs=placed,
         out_specs=(

time: 363 us -> 114 us (0.31)
  the two profiles are of different devices: /device:TPU:13 before, /device:TPU:0 now
where the time goes in v1:
time: 114 us
  Pallas kernels  106 us (93%)
  local copies, waits for them, and re-layouts  6.95 us (6%)
    pallas_call x1, Pallas kernels, local_tree(): pl.pallas_call(functools.partial(layer_kernel, cap), out_shape=(jax.Shape...  106 us
    unnamed x19, local copies, waits for them, and re-layouts  6.95 us

profile of v1, /device:TPU:0, one launch (start us, length us, event | category | flops | bytes accessed | tf_op | source)
XLA Modules:
  0.0 114.1 jit_solution(12101718567925384006)
XLA Ops:
  0.6 0.0 copy-start.7
  0.6 0.0 copy-start.4
  0.7 0.0 copy-start.5
  0.7 0.0 copy-start.6
  0.7 0.6 copy-done.7
  1.3 0.0 copy-done.4
  1.3 0.0 copy-done.5
  1.3 0.0 copy-done.6
  1.3 0.0 copy-start
  1.3 1.2 %copy-done = bf16[1,3584,128]{2,1,0:T(8,128)(2,1)S(1)} copy-done((bf16[1,3584,128]{2,1,0:T(8,128)(2,1)S(1)}, bf16[1,3584,128]{2,1,0:T(8,128)(2,1)}, u32[]{:S(2)}) %copy-start) | copy-done | bytes 917528
  2.5 0.0 copy-start.1
  2.5 1.0 copy-done.1
  3.5 0.0 copy-start.2
  3.5 1.0 copy-done.2
  4.6 0.0 copy-start.3
  4.6 1.0 copy-done.3
  5.6 106.5 %shard_map.121 = (bf16[64,3584]{1,0:T(8,128)(2,1)S(1)}, bf16[64,3584]{1,0:T(8,128)(2,1)S(1)}, f32[1,64]{1,0:T(1,128)S(1)}) custom-call(bf16[64,3584]{1,0:T(8,128)(2,1)S(1)} %bitcast.11, s32[1,64]{1,0:T(1,128)S(1)} %copy-done.4, f32[1,64]{1,0:T(1,128)S(1)} %copy-done.5, bf16[64,3584]{1,0:T(8,128)(2,1)S(1)} %bitcast.12, bf16[64,3584]{1,0:T(8,128)(2,1)S(1)} %bitcast.13, ...), custom_call_target="tpu_custom_call" | custom-call | flops 2818572288 | bytes 6000000 | tf_op jit(solution)/shard_map/pallas_call | solution.py:495
  112.1 0.8 copy.16
  112.8 0.8 copy.17
  113.6 0.5 copy.18
Async XLA Ops:
  0.6 0.7 copy-start.7
  0.6 0.7 copy-start.4
  0.7 0.7 copy-start.5
  0.7 0.7 copy-start.6
  1.3 1.2 %copy-start = (bf16[1,3584,128]{2,1,0:T(8,128)(2,1)S(1)}, bf16[1,3584,128]{2,1,0:T(8,128)(2,1)}, u32[]{:S(2)}) copy-start(bf16[1,3584,128]{2,1,0:T(8,128)(2,1)} %param.17) | copy-start | bytes 2752516
  2.5 1.0 copy-start.1
  3.5 1.0 copy-start.2
  4.6 1.0 copy-start.3

commit v2 on v0

--- a/solution.py
+++ b/solution.py
@@ -1,6 +1,10 @@
+import functools
+
 import jax
 import jax.numpy as jnp
 from jax import lax
+from jax.experimental import pallas as pl
+from jax.experimental.pallas import tpu as pltpu
 from jax.sharding import PartitionSpec as P
 
 FF = 1024
@@ -118,6 +122,443 @@
     return (mixed[None], input_grad[None], gate_grad[None])
 
 
+MESH = pl.DeviceIdType.MESH
+X, F, G = 0, 1, 2
+HALF_STEP = 256
+
+
+def flip(index, bit):
+    return index + bit - 2 * bit * lax.rem(lax.div(index, bit), 2)
+
+
+def make_plan(route_row, own_expert, capacity):
+    count = route_row.shape[1]
+    row = route_row.astype(jnp.float32)
+    at_row = lax.broadcasted_iota(jnp.int32, (count, count), 0)
+    at_col = lax.broadcasted_iota(jnp.int32, (count, count), 1)
+    wide = jnp.broadcast_to(row, (count, count))
+    col = jnp.sum(jnp.where(at_row == at_col, wide, 0.0), axis=1, keepdims=True)
+    same = jnp.where(wide == col, 1.0, 0.0)
+    slot_col = jnp.sum(jnp.where(at_col < at_row, same, 0.0), axis=1, keepdims=True)
+    slot_row = jnp.sum(jnp.where(at_row < at_col, same, 0.0), axis=0, keepdims=True)
+    own = own_expert.astype(jnp.float32)
+
+    def onehot(shape, axis, route, slot):
+        at = lax.broadcasted_iota(jnp.int32, shape, axis).astype(jnp.float32)
+        first = at < capacity
+        expert = jnp.where(first, own, 1.0 - own)
+        place = jnp.where(first, at, at - capacity)
+        hit = jnp.where(route == expert, 1.0, 0.0) * jnp.where(slot == place, 1.0, 0.0)
+        return hit.astype(jnp.bfloat16)
+
+    pick = onehot((2 * capacity, count), 0, row, slot_row)
+    spread = onehot((count, 2 * capacity), 1, col, slot_col)
+    return pick, spread
+
+
+def as_column(row):
+    count = row.shape[1]
+    at_row = lax.broadcasted_iota(jnp.int32, (count, count), 0)
+    at_col = lax.broadcasted_iota(jnp.int32, (count, count), 1)
+    wide = jnp.broadcast_to(row, (count, count))
+    return jnp.sum(jnp.where(at_row == at_col, wide, 0.0), axis=1, keepdims=True)
+
+
+def as_row(col):
+    count = col.shape[0]
+    at_row = lax.broadcasted_iota(jnp.int32, (count, count), 0)
+    at_col = lax.broadcasted_iota(jnp.int32, (count, count), 1)
+    wide = jnp.broadcast_to(col, (count, count))
+    return jnp.sum(jnp.where(at_row == at_col, wide, 0.0), axis=0, keepdims=True)
+
+
+def dot(a, b):
+    return jnp.dot(a, b, preferred_element_type=jnp.float32)
+
+
+def dot_t(a, b):
+    return lax.dot_general(a, b, (((1,), (1,)), ((), ())), preferred_element_type=jnp.float32)
+
+
+def layer_kernel(
+    capacity,
+    fa, fr_hbm, fw_hbm, ba_hbm, bg, br_hbm, bw_hbm, wg_hbm, wu_hbm, wd_hbm,
+    mixed, in_grad, gate_grad,
+    fr, fw, br, bw, xb, xf, xg, fold_s, rows, wgu, wd, pre_x, pre_f, hid, dd,
+    part_f, part_x, core_f, core_x, two_f, two_x, one_f, one_x, last_s, last_r, own_s,
+    w_sem, relay_s, relay_r, mir_s, mir_r, row_s, row_r, c_s, c_r, t_s, t_r, o_s, o_r, l_s, l_r,
+):
+    depth = xb.shape[1]
+    half = depth // 2
+    unit = wd.shape[0] // 2
+    cap = capacity
+    section = lax.axis_index("section")
+    me = lax.axis_index("expert")
+    core = lax.rem(me, 2)
+    j = lax.rem(me, 8)
+    base = me - j
+    across, along = flip(j, 4), flip(j, 2)
+    first = (across, (1 - core) * across + core * along)
+    second = (along, (1 - core) * along + core * across)
+    corner = flip(across, 2)
+    other = flip(j, 1)
+
+    def in_group(k):
+        return (section, base + k)
+
+    mirror = (section, flip(me, 8))
+    relay = (1 - section, me)
+    loads = [
+        pltpu.make_async_copy(src, dst, w_sem.at[k])
+        for k, (src, dst) in enumerate(
+            (
+                (ba_hbm, xb),
+                (br_hbm, br),
+                (fr_hbm, fr),
+                (bw_hbm, bw),
+                (fw_hbm, fw),
+                (wg_hbm.at[pl.ds(0, half)], wgu.at[:, pl.ds(0, unit)]),
+                (wu_hbm.at[pl.ds(0, half)], wgu.at[:, pl.ds(unit, unit)]),
+                (wg_hbm.at[pl.ds(half, half)], wgu.at[:, pl.ds(2 * unit, unit)]),
+                (wu_hbm.at[pl.ds(half, half)], wgu.at[:, pl.ds(3 * unit, unit)]),
+                (wd_hbm.at[:, pl.ds(0, half)], wd.at[pl.ds(0, unit)]),
+                (wd_hbm.at[:, pl.ds(half, half)], wd.at[pl.ds(unit, unit)]),
+            )
+        )
+    ]
+    for load in loads:
+        load.start()
+    barrier = pltpu.get_barrier_semaphore()
+    for target in (relay, mirror, in_group(across), in_group(along), in_group(other)):
+        pl.semaphore_signal(barrier, inc=1, device_id=target, device_id_type=MESH)
+    pl.semaphore_wait(barrier, 5)
+
+    def remote(src, dst, send, recv, target):
+        return pltpu.make_async_remote_copy(
+            src_ref=src, dst_ref=dst, send_sem=send, recv_sem=recv,
+            device_id=target, device_id_type=MESH,
+        )
+
+    sent = []
+
+    def go(copy):
+        copy.start()
+        sent.append(copy)
+
+    relay_f = remote(fa, xf, relay_s.at[0], relay_r.at[0], relay)
+    relay_g = remote(bg, xg, relay_s.at[1], relay_r.at[1], relay)
+    relay_f.start()
+    for load in loads[:5]:
+        load.wait()
+    own_expert = lax.div(me, 8)
+    pick_b, spread_b = make_plan(br[...], own_expert, cap)
+    pick_f, spread_f = make_plan(fr[...], own_expert, cap)
+    picks = (pick_b, pick_f, pick_b)
+    sources = (xb, xf, xg)
+
+    def halves(k):
+        lo = pl.ds(pl.multiple_of(k * HALF_STEP, HALF_STEP), HALF_STEP)
+        hi = pl.ds(pl.multiple_of(half + k * HALF_STEP, HALF_STEP), HALF_STEP)
+        return lo, hi
+
+    def mirror_copy(t):
+        return remote(fold_s.at[t], rows.at[t, 1, j], mir_s.at[t], mir_r.at[t], mirror)
+
+    def row_copy(t, m, slot, send_at, target):
+        block = rows.at[t, m, slot]
+        return remote(
+            block, block, row_s.at[t, m, send_at], row_r.at[t, m, slot], in_group(target)
+        )
+
+    def send_block(t, m):
+        go(row_copy(t, m, j, 0, first[m]))
+        go(row_copy(t, m, j, 1, second[m]))
+        go(row_copy(t, m, j, 2, other))
+
+    def pack(t):
+        @pl.loop(0, half // HALF_STEP)
+        def _(k):
+            lo, hi = halves(k)
+            left, right = dot(picks[t], sources[t][:, lo]), dot(picks[t], sources[t][:, hi])
+            fold_s[t, :, lo] = jnp.concatenate([left[cap:], right[cap:]], axis=0).astype(
+                jnp.bfloat16
+            )
+            rows[t, 0, j, :, lo] = jnp.concatenate([left[:cap], right[:cap]], axis=0).astype(
+                jnp.bfloat16
+            )
+
+        go(mirror_copy(t))
+        send_block(t, 0)
+
+    def mirror_in(t):
+        mirror_copy(t).wait_recv()
+        send_block(t, 1)
+
+    def forward_first(t, m):
+        row_copy(t, m, first[m], 3, second[m]).wait_recv()
+        go(row_copy(t, m, first[m], 3, second[m]))
+        go(row_copy(t, m, first[m], 4, other))
+
+    def forward_second(t, m):
+        for slot, at in ((second[m], 5), (corner, 6)):
+            row_copy(t, m, slot, at, other).wait_recv()
+            go(row_copy(t, m, slot, at, other))
+
+    def gathered(t, m):
+        for k in range(4):
+            row_copy(t, m, 2 * k + 1 - core, 0, other).wait_recv()
+
+    def unfold(value, width):
+        blocks = value.reshape(8, 2 * cap, 2 * width)
+        return (blocks[:, :cap, :width] + blocks[:, cap:, width:]).reshape(8 * cap, width)
+
+    def gate_up(t, m, out):
+        gathered(t, m)
+        out[m] = unfold(dot(rows[t, m].reshape(16 * cap, half), wgu[...]), 2 * unit)
+
+    def fold(left, right):
+        width = left.shape[1]
+        both = [left.reshape(8, cap, width), right.reshape(8, cap, width)]
+        return jnp.concatenate(both, axis=1).astype(jnp.bfloat16)
+
+    def forward_out(m):
+        gate = pre_f[m, :, :unit]
+        up = pre_f[m, :, unit:]
+        hid[m] = (gate * jax.nn.sigmoid(gate) * up).astype(jnp.bfloat16)
+
+        @pl.loop(0, half // HALF_STEP)
+        def _(k):
+            lo, _ = halves(k)
+            part_f[m, :, :, lo] = fold(dot(hid[m], wd[:unit, lo]), dot(hid[m], wd[unit:, lo]))
+
+        send_core(0, m)
+
+    def backward_out(m):
+        gathered(G, m)
+        grad = unfold(dot_t(rows[G, m].reshape(16 * cap, half), wd[...]), unit)
+        gate = pre_x[m, :, :unit]
+        up = pre_x[m, :, unit:]
+        sig = jax.nn.sigmoid(gate)
+        active = gate * sig
+        hidden = (active * up).astype(jnp.bfloat16).astype(jnp.float32)
+        dd[m, :, :unit] = (grad * up * sig * (1.0 + gate * (1.0 - sig))).astype(jnp.bfloat16)
+        dd[m, :, unit:] = (grad * active).astype(jnp.bfloat16)
+        term = jnp.broadcast_to(jnp.sum(hidden * grad, axis=1, keepdims=True), (8 * cap, 128))
+        part_x[m, :, :, pl.ds(half, 128)] = fold(term, term)
+
+        @pl.loop(0, half // HALF_STEP)
+        def _(k):
+            lo, _ = halves(k)
+            part_x[m, :, :, lo] = fold(
+                dot_t(dd[m], wgu[lo, : 2 * unit]), dot_t(dd[m], wgu[lo, 2 * unit :])
+            )
+
+        send_core(1, m)
+
+    parts, cores = (part_f, part_x), (core_f, core_x)
+    twos, ones = (two_f, two_x), (one_f, one_x)
+
+    def core_copy(o, m, k):
+        return remote(
+            parts[o].at[m, 2 * k + 1 - core], cores[o].at[m, k],
+            c_s.at[o, m, k], c_r.at[o, m, k], in_group(other),
+        )
+
+    def two_copy(o, m, k):
+        return remote(
+            parts[o].at[m, (second[m], corner)[k]], twos[o].at[m, k],
+            t_s.at[o, m, k], t_r.at[o, m, k], in_group(second[m]),
+        )
+
+    def one_copy(o, m):
+        return remote(
+            parts[o].at[m, first[m]], ones[o].at[m], o_s.at[o, m], o_r.at[o, m],
+            in_group(first[m]),
+        )
+
+    def last_copy(o):
+        return remote(last_s.at[o], last_r.at[o], l_s.at[o], l_r.at[o], mirror)
+
+    def send_core(o, m):
+        for k in range(4):
+            go(core_copy(o, m, k))
+
+    def add_into(ref, m, slot, box):
+        ref[m, slot] = (
+            ref[m, slot].astype(jnp.float32) + box.astype(jnp.float32)
+        ).astype(jnp.bfloat16)
+
+    def merge_core(o, m):
+        for k in range(4):
+            core_copy(o, m, k).wait_recv()
+
+        @pl.loop(0, 4)
+        def _(k):
+            add_into(parts[o], m, 2 * k + core, cores[o][m, k])
+
+        go(two_copy(o, m, 1))
+        go(two_copy(o, m, 0))
+
+    def merge_two(o, m):
+        two_copy(o, m, 1).wait_recv()
+        add_into(parts[o], m, first[m], twos[o][m, 1])
+        go(one_copy(o, m))
+        two_copy(o, m, 0).wait_recv()
+        add_into(parts[o], m, j, twos[o][m, 0])
+
+    def merge_one(o, m):
+        one_copy(o, m).wait_recv()
+        width = parts[o].shape[-1]
+        value = parts[o][m, j].astype(jnp.float32) + ones[o][m].astype(jnp.float32)
+        target = (own_s, last_s)[m]
+        target[o, :, :width] = value.astype(jnp.bfloat16)
+        if width < target.shape[-1]:
+            rest = (value.shape[0], target.shape[-1] - width)
+            target[o, :, width:] = jnp.zeros(rest, jnp.bfloat16)
+        if m == 1:
+            go(last_copy(o))
+
+    def finish(o, spread, weight_row, base_rows, out):
+        last_copy(o).wait_recv()
+        weight = as_column(weight_row)
+
+        def spread_sums(cols):
+            near = own_s[o, :, cols].astype(jnp.float32)
+            far = last_r[o, :, cols].astype(jnp.float32)
+            left = jnp.concatenate([near[:cap], far[:cap]], axis=0).astype(jnp.bfloat16)
+            right = jnp.concatenate([near[cap:], far[cap:]], axis=0).astype(jnp.bfloat16)
+            return dot(spread, left), dot(spread, right)
+
+        @pl.loop(0, half // HALF_STEP)
+        def _(k):
+            lo, hi = halves(k)
+            for cols, value in zip((lo, hi), spread_sums(lo)):
+                out[:, cols] = (
+                    base_rows[:, cols].astype(jnp.float32) + weight * value
+                ).astype(jnp.bfloat16)
+
+        if o == 1:
+            value, _ = spread_sums(pl.ds(half, 128))
+            gate_grad[...] = as_row(value[:, :1])
+
+    pack(X)
+    forward_first(X, 0)
+    mirror_in(X)
+    relay_f.wait_recv()
+    relay_f.wait_send()
+    relay_g.start()
+    pack(F)
+    forward_first(X, 1)
+    forward_second(X, 0)
+    mirror_in(F)
+    forward_first(F, 0)
+    forward_second(X, 1)
+    for load in loads[5:]:
+        load.wait()
+    gate_up(X, 0, pre_x)
+    relay_g.wait_recv()
+    pack(G)
+    forward_first(F, 1)
+    forward_second(F, 0)
+    gate_up(X, 1, pre_x)
+    mirror_in(G)
+    forward_first(G, 0)
+    forward_second(F, 1)
+    gate_up(F, 0, pre_f)
+    gate_up(F, 1, pre_f)
+    forward_out(1)
+    forward_first(G, 1)
+    forward_out(0)
+    forward_second(G, 0)
+    merge_core(0, 1)
+    merge_core(0, 0)
+    forward_second(G, 1)
+    backward_out(1)
+    backward_out(0)
+    merge_two(0, 1)
+    merge_core(1, 1)
+    merge_core(1, 0)
+    merge_two(0, 0)
+    merge_one(0, 1)
+    merge_two(1, 1)
+    merge_one(0, 0)
+    merge_two(1, 0)
+    merge_one(1, 1)
+    finish(0, spread_f, fw[...], xf, mixed)
+    merge_one(1, 0)
+    finish(1, spread_b, bw[...], xg, in_grad)
+    relay_g.wait_send()
+    for copy in sent:
+        copy.wait_send()
+
+
+def local_tree(
+    fwd_act, fwd_route, fwd_weight, bwd_act, bwd_grad, bwd_route, bwd_weight, w_gate, w_up, w_down
+):
+    count, depth = fwd_act.shape[1:]
+    unit = w_gate.shape[2]
+    cap = 3 * count // 8
+    pair = 2 * cap
+    half = depth // 2
+    wide = half + 128
+    bf16, f32, i32 = jnp.bfloat16, jnp.float32, jnp.int32
+    vmem = pl.BlockSpec(memory_space=pltpu.VMEM)
+    hbm = pl.BlockSpec(memory_space=pl.ANY)
+    dma = pltpu.SemaphoreType.DMA
+    buf = pltpu.VMEM
+    mixed, in_grad, gate_grad = pl.pallas_call(
+        functools.partial(layer_kernel, cap),
+        out_shape=(
+            jax.ShapeDtypeStruct((count, depth), bf16),
+            jax.ShapeDtypeStruct((count, depth), bf16),
+            jax.ShapeDtypeStruct((1, count), f32),
+        ),
+        in_specs=[hbm] * 10,
+        out_specs=(vmem, vmem, vmem),
+        scratch_shapes=[
+            buf((1, count), i32),
+            buf((1, count), f32),
+            buf((1, count), i32),
+            buf((1, count), f32),
+            buf((count, depth), bf16),
+            buf((count, depth), bf16),
+            buf((count, depth), bf16),
+            buf((3, pair, half), bf16),
+            buf((3, 2, 8, pair, half), bf16),
+            buf((half, 4 * unit), bf16),
+            buf((2 * unit, half), bf16),
+            buf((2, 8 * cap, 2 * unit), f32),
+            buf((2, 8 * cap, 2 * unit), f32),
+            buf((2, 8 * cap, unit), bf16),
+            buf((2, 8 * cap, 2 * unit), bf16),
+            buf((2, 8, pair, half), bf16),
+            buf((2, 8, pair, wide), bf16),
+            buf((2, 4, pair, half), bf16),
+            buf((2, 4, pair, wide), bf16),
+            buf((2, 2, pair, half), bf16),
+            buf((2, 2, pair, wide), bf16),
+            buf((2, pair, half), bf16),
+            buf((2, pair, wide), bf16),
+            buf((2, pair, wide), bf16),
+            buf((2, pair, wide), bf16),
+            buf((2, pair, wide), bf16),
+            dma((11,)), dma((2,)), dma((2,)), dma((3,)), dma((3,)),
+            dma((3, 2, 7)), dma((3, 2, 8)), dma((2, 2, 4)), dma((2, 2, 4)),
+            dma((2, 2, 2)), dma((2, 2, 2)), dma((2, 2)), dma((2, 2)), dma((2,)), dma((2,)),
+        ],
+        compiler_params=pltpu.CompilerParams(
+            collective_id=0, has_side_effects=True, vmem_limit_bytes=58 * 1024 * 1024
+        ),
+        cost_estimate=pl.CostEstimate(
+            flops=2 * 8 * 8 * pair * depth * unit, bytes_accessed=6_000_000, transcendentals=100_000
+        ),
+    )(
+        fwd_act[0], fwd_route, fwd_weight, bwd_act[0], bwd_grad[0], bwd_route, bwd_weight,
+        w_gate[0], w_up[0], w_down[0],
+    )
+    return (mixed[None], in_grad[None], gate_grad)
+
+
 def solution(mesh):
     placed = (
         P("section", "expert", None),
@@ -131,8 +572,9 @@
         P("section", None, "expert"),
         P("section", "expert", None),
     )
+    pair_of_experts = mesh.shape["section"] == 2 and mesh.shape["expert"] == 16
     return jax.shard_map(
-        local,
+        local_tree if pair_of_experts else local,
         mesh=mesh,
         in_specs=placed,
         out_specs=(

time: 363 us -> 93.9 us (0.26)
  the two profiles are of different devices: /device:TPU:13 before, /device:TPU:0 now
where the time goes in v2:
time: 93.9 us; the launch traced here: 93.7 us
  Pallas kernels  89.9 us (96%)
  local copies, waits for them, and re-layouts  3.15 us (3%)
    pallas_call x1, Pallas kernels, local_tree(): pl.pallas_call(functools.partial(layer_kernel, cap), out_shape=(jax.Shape...  89.9 us
    unnamed x7, local copies, waits for them, and re-layouts  3.15 us

profile of v2, /device:TPU:0, one launch (start us, length us, event | category | flops | bytes accessed | tf_op | source)
XLA Modules:
  0.0 93.7 jit_solution(15200936359277903423)
XLA Ops:
  0.6 89.9 %shard_map.121 = (bf16[64,3584]{1,0:T(8,128)(2,1)}, bf16[64,3584]{1,0:T(8,128)(2,1)}, f32[1,64]{1,0:T(1,128)}) custom-call(bf16[64,3584]{1,0:T(8,128)(2,1)} %bitcast.13, s32[1,64]{1,0:T(1,128)} %fr_hbm.1, f32[1,64]{1,0:T(1,128)} %fw_hbm.1, bf16[64,3584]{1,0:T(8,128)(2,1)} %bitcast.14, bf16[64,3584]{1,0:T(8,128)(2,1)} %bitcast.15, s32[1,64]{1,0:T(1,128)} %br_hbm.1, ...), custom_call_target="tpu_custom_call" | custom-call | flops 2818572288 | bytes 6000000 | tf_op jit(solution)/shard_map/pallas_call | solution.py:509
  90.5 0.0 copy-start
  90.6 1.9 %copy.16 = bf16[1,64,3584]{2,1,0:T(8,128)(2,1)} copy(bf16[1,64,3584]{2,1,0:T(8,128)(2,1)} %bitcast.9) | data formatting | bytes 917504
  92.4 0.0 copy-done
  92.4 0.0 copy-start.1
  92.4 0.8 copy.17
  93.2 0.0 copy-done.1
  93.2 0.5 copy.18
Async XLA Ops:
  90.5 1.9 %copy-start = (bf16[64,3584]{1,0:T(8,128)(2,1)S(1)}, bf16[64,3584]{1,0:T(8,128)(2,1)}, u32[]{:S(2)}) copy-start(bf16[64,3584]{1,0:T(8,128)(2,1)} %get-tuple-element.7) | copy-start | bytes 1376260
  92.4 0.8 copy-start.1
